TPU v7x, 512 devices: a whole 4x4x16 slice. The times are simulated.
512 devices in a mesh: ed: 64 (over z, x_hi, core), tp: 8 (over y, x_lo).
Axes of the slice: x: 4 (x_hi: 2, x_lo: 2; x = x_hi * 2 + x_lo), y: 4, z: 16, core: 2. Of those that a mesh axis runs over, the one named last changes fastest.
Arguments:
- tokens: bfloat16 [8192, 3072], P('ed', 'tp'), may hold values from -6 to 6
- gate_weight: bfloat16 [64, 3072, 2048], P('ed', None, 'tp'), as said below
- up_weight: bfloat16 [64, 3072, 2048], P('ed', None, 'tp'), as said below
- experts: int32 [8192, 2], P('ed'), may hold values from 0 to 7, as said below
- placement: int32 [16], replicated, may hold values from 0 to 7, as said below
- mix_weight: float32 [8192, 2], P('ed'), may hold values from 0.1 to 1
Outputs:
- expert_out: bfloat16 [8192, 2, 8192], P('ed', None, 'tp')
Inputs may be any that keep to these rules, and one draw needn't show every extreme that they name: Each token names two different experts. In each aligned block of 128 tokens, at most 32 times the number of slots holding e of the block's choices name expert e, and some expert held by one slot is named exactly 32 times. `placement`: never falls; every expert is held by 1 to 6 slots. `gate_weight`: rows s * 4 + g and r * 4 + g are equal whenever placement[s] = placement[r]. `up_weight`: rows s * 4 + g and r * 4 + g are equal whenever placement[s] = placement[r].
All inputs are finite; a program needn't handle non-finite values.
Results may differ from a plain program's by a relative error of at most 0.0049.
Values may be sent and summed in bfloat16 or wider, within the bound.
A program may use at most 64 MiB of HBM per device.

v0:
```python
import jax
import jax.numpy as jnp
from jax import lax
from jax.sharding import PartitionSpec as P

EXPERTS = 8
MOST = 32


def assign_slots(experts, placement):
    chosen_flat = experts.reshape(-1)
    expert_range = jnp.arange(EXPERTS, dtype=jnp.int32)
    holders = (placement[:, None] == expert_range[None, :]).astype(jnp.int32)
    replicas = jnp.sum(holders, axis=0)
    first_slot = jnp.sum((placement[:, None] < expert_range[None, :]).astype(jnp.int32), axis=0)
    chosen = (chosen_flat[:, None] == expert_range[None, :]).astype(jnp.int32)
    earlier = jnp.cumsum(chosen, axis=0) - chosen
    rank_index = jnp.sum(earlier * chosen, axis=1)
    replica_count = jnp.sum(chosen * replicas[None, :], axis=1)
    slot_start = jnp.sum(chosen * first_slot[None, :], axis=1)
    slot_index = slot_start + rank_index % replica_count
    position = rank_index // replica_count
    return (slot_index, position)


def hidden_units(row_block, gate_local, up_local):
    gate_sum = jnp.dot(row_block, gate_local, preferred_element_type=jnp.float32)
    up_sum = jnp.dot(row_block, up_local, preferred_element_type=jnp.float32)
    return (jax.nn.silu(gate_sum) * up_sum).astype(jnp.bfloat16)


def return_rows(hidden):
    return lax.all_to_all(hidden, "ed", split_axis=0, concat_axis=0, tiled=True)


def body(tokens, gate_weight, up_weight, experts, placement, mix_weight):
    tok_rows = tokens.shape[0]
    top_count = experts.shape[1]
    slot_total = placement.shape[0]
    axis_width = lax.axis_size("ed")
    group_size = axis_width // slot_total
    gate_local = gate_weight[0]
    up_local = up_weight[0]
    slot_index, position = assign_slots(experts, placement)
    token_rows = lax.all_gather(tokens, "tp", axis=1, tiled=True)
    feature_width = token_rows.shape[1]
    pair_rows = jnp.repeat(token_rows, top_count, axis=0)
    slot_buffer = (
        jnp.zeros((slot_total * MOST, feature_width), jnp.bfloat16)
        .at[slot_index * MOST + position]
        .set(pair_rows)
    )
    outgoing = jnp.broadcast_to(
        slot_buffer.reshape(slot_total, 1, MOST, feature_width),
        (slot_total, group_size, MOST, feature_width),
    ).reshape(axis_width, MOST, feature_width)
    arrived = lax.all_to_all(outgoing, "ed", split_axis=0, concat_axis=0, tiled=True)
    sources = arrived.shape[0]
    item_count = arrived.shape[1]
    hidden = hidden_units(
        arrived.reshape(sources * item_count, feature_width), gate_local, up_local
    )
    returned = return_rows(hidden.reshape(sources, item_count, hidden.shape[1]))
    unit_count = returned.shape[2]
    by_slot = returned.reshape(slot_total, group_size, MOST, unit_count)
    gathered = by_slot[slot_index, :, position]
    pair_hidden = gathered.reshape(tok_rows * top_count, group_size * unit_count)
    weighted = pair_hidden.astype(jnp.float32) * mix_weight.reshape(-1)[:, None]
    return weighted.astype(jnp.bfloat16).reshape(tok_rows, top_count, group_size * unit_count)


def solution(mesh):
    placed = (
        P("ed", "tp"),
        P("ed", None, "tp"),
        P("ed", None, "tp"),
        P("ed", None),
        P(),
        P("ed", None),
    )
    return jax.shard_map(
        body, mesh=mesh, in_specs=placed, out_specs=P("ed", None, "tp"), check_vma=False
    )
```

profile of v0, /device:TPU:1, one launch (start us, length us, event | category | flops | bytes accessed | tf_op | source)
XLA Modules:
  0.0 695.8 jit_solution(10466984101981294726)
XLA Ops:
  0.0 0.0 copy-start
  0.0 0.9 copy.15
  0.9 0.1 eq.53
  1.0 0.1 eq.49
  1.2 0.6 reduce-window.6
  1.8 0.2 slice_reduce_fusion
  2.0 0.8 convert_reduce_fusion.1
  2.9 27.1 %all_gather.3 = bf16[128,3072]{1,0:T(8,128)(2,1)S(1)} all-gather(bf16[128,384]{1,0:T(8,128)(2,1)} %param.6), channel_id=1, replica_groups=mesh['ed'=64,'tp'=8] {'tp'}, dimensions={1}, use_global_device_ids=true | all-gather | bytes 884736 | tf_op jit(solution)/shard_map/all_gather | solution.py:45
  30.0 0.8 broadcast_in_dim.14
  30.8 1.5 reshape.190
  32.3 0.1 select_reduce_fusion.1
  32.4 0.2 fusion.12
  32.6 5.8 scatter_custom_fusion
  38.4 8.1 %broadcast_in_dim.16 = bf16[16,4,32,3072]{3,2,1,0:T(8,128)(2,1)} broadcast(bf16[16,32,3072]{2,1,0:T(8,128)(2,1)} %bitcast.30), dimensions={0,2,3} | broadcast | bytes 15728640 | tf_op jit(solution)/shard_map/broadcast_in_dim | solution.py:53
  46.5 571.9 %all_to_all.10 = bf16[64,32,3072]{2,1,0:T(8,128)(2,1)S(1)} all-to-all(bf16[64,32,3072]{2,1,0:T(8,128)(2,1)} %bitcast.26), channel_id=1, replica_groups=mesh['ed'=64,'tp'=8] {'ed'}, dimensions={0} | all-to-all | bytes 25165824 | tf_op jit(solution)/shard_map/all_to_all | solution.py:57
  618.4 0.0 copy-done
  618.4 0.0 copy-start.2
  618.4 3.7 fusion.2
  622.1 0.0 copy-done.2
  622.1 5.1 fusion
  627.2 0.0 copy-start.1
  627.2 8.1 %all-to-all-start.1 = ((bf16[64,32,256]{2,1,0:T(8,128)(2,1)}), bf16[64,32,256]{2,1,0:T(8,128)(2,1)S(1)}, u32[]{:S(2)}, u32[]{:S(2)}) async-start(bf16[64,32,256]{2,1,0:T(8,128)(2,1)} %bitcast.32), calls=%async_computation.1 | async-start | bytes 2097152 | tf_op jit(solution)/shard_map/all_to_all | solution.py:33
  635.3 0.0 copy-done.1
  635.3 0.1 copy.18
  635.4 53.9 %all-to-all-done.1 = bf16[64,32,256]{2,1,0:T(8,128)(2,1)S(1)} async-done(((bf16[64,32,256]{2,1,0:T(8,128)(2,1)}), bf16[64,32,256]{2,1,0:T(8,128)(2,1)S(1)}, u32[]{:S(2)}, u32[]{:S(2)}) %all-to-all-start.1) | async-done | bytes 1048608 | tf_op jit(solution)/shard_map/all_to_all | solution.py:33
  689.4 1.9 copy.17
  691.2 2.7 gather_fusion
  694.0 0.6 reshape.179
  694.6 1.2 multiply_convert_fusion
  (4 shorter events, 0.1 us)
Async XLA Ops:
  0.0 618.4 %copy-start = (bf16[1,3072,256]{2,1,0:T(8,128)(2,1)S(1)}, bf16[1,3072,256]{2,1,0:T(8,128)(2,1)}, u32[]{:S(2)}) copy-start(bf16[1,3072,256]{2,1,0:T(8,128)(2,1)} %param.7) | copy-start | bytes 4718596
  618.4 3.7 copy-start.2
  627.2 8.1 %copy-start.1 = (f32[128,2]{0,1:T(2,128)S(1)}, f32[128,2]{0,1:T(2,128)}, u32[]{:S(2)}) copy-start(f32[128,2]{0,1:T(2,128)} %param.11) | copy-start | bytes 3076
  627.2 62.1 %all-to-all-start.1 = ((bf16[64,32,256]{2,1,0:T(8,128)(2,1)}), bf16[64,32,256]{2,1,0:T(8,128)(2,1)S(1)}, u32[]{:S(2)}, u32[]{:S(2)}) async-start(bf16[64,32,256]{2,1,0:T(8,128)(2,1)} %bitcast.32), calls=%async_computation.1 | async-start | bytes 2097152 | tf_op jit(solution)/shard_map/all_to_all | solution.py:33
where the time goes:
time: 698 us; the launch traced here: 696 us
  blocking collectives  599 us (86%)
  waiting for transfers between devices  53.9 us (8%)
  local copies, waits for them, and re-layouts  22.9 us (3%)
  matrix products  8.8 us (1%)
  starting transfers between devices  8.08 us (1%)
    all_to_all x1, blocking collectives, body(): lax.all_to_all(outgoing, 'ed', split_axis=0, concat_axis=0, tiled=True)  572 us
    all_to_all x1, waiting for transfers between devices, return_rows(): return lax.all_to_all(hidden, 'ed', split_axis=0, concat_axis=0, tiled=True)  53.9 us
    all_gather x1, blocking collectives, body(): token_rows = lax.all_gather(tokens, 'tp', axis=1, tiled=True)  27.1 us
  transfers between devices with their start and end apart: 1, of which 1 were waited for; matrix products, arithmetic and copies ran while one was open for 0% of the time, Pallas kernels for 0%

commit v1 on v0

v1 whole, which is shorter than its diff:
```python
import jax
import jax.numpy as jnp
from jax import lax
from jax.sharding import Mesh, PartitionSpec as P

EXPERTS = 8
MOST = 32
PLANE = ("xh", "core", "y", "xl")
ED = ("z", "xh", "core")


def assign_slots(experts, placement):
    chosen_flat = experts.reshape(-1)
    expert_range = jnp.arange(EXPERTS, dtype=jnp.int32)
    holders = (placement[:, None] == expert_range[None, :]).astype(jnp.int32)
    replicas = jnp.sum(holders, axis=0)
    first_slot = jnp.sum((placement[:, None] < expert_range[None, :]).astype(jnp.int32), axis=0)
    chosen = (chosen_flat[:, None] == expert_range[None, :]).astype(jnp.int32)
    earlier = jnp.cumsum(chosen, axis=0) - chosen
    rank_index = jnp.sum(earlier * chosen, axis=1)
    replica_count = jnp.sum(chosen * replicas[None, :], axis=1)
    slot_start = jnp.sum(chosen * first_slot[None, :], axis=1)
    slot_index = slot_start + rank_index % replica_count
    position = rank_index // replica_count
    return (slot_index, position)


def body(tokens, gate_weight, up_weight, experts, placement, mix_weight):
    tok_rows, width = tokens.shape
    top = experts.shape[1]
    slots = placement.shape[0]
    slot_index, position = assign_slots(experts, placement)
    place = slot_index * MOST + position
    spots = jnp.arange(slots * MOST, dtype=jnp.int32)
    pick = (place[:, None] == spots[None, :]).astype(jnp.bfloat16)
    spread = jnp.sum(pick.reshape(tok_rows, top, slots * MOST), axis=1)
    rows = lax.dot_general(
        spread, tokens, (((0,), (0,)), ((), ())), preferred_element_type=jnp.float32
    ).astype(jnp.bfloat16)
    arrived = lax.all_to_all(
        rows.reshape(slots, MOST, width), "z", split_axis=0, concat_axis=0, tiled=True
    ).reshape(slots * MOST, width)
    whole = lax.all_gather(arrived, PLANE, axis=0, tiled=False)
    whole = whole.reshape(4, 8, slots, MOST, width).transpose(2, 0, 3, 1, 4)
    whole = whole.reshape(slots * 4 * MOST, 8 * width)
    gate_sum = jnp.dot(whole, gate_weight[0], preferred_element_type=jnp.float32)
    up_sum = jnp.dot(whole, up_weight[0], preferred_element_type=jnp.float32)
    hidden = (jax.nn.silu(gate_sum) * up_sum).astype(jnp.bfloat16)
    units = hidden.shape[1]
    returned = lax.all_to_all(
        hidden.reshape(slots * 4, MOST, units), ED, split_axis=0, concat_axis=0, tiled=True
    )
    by_row = returned.reshape(slots, 4, MOST, units).transpose(0, 2, 1, 3)
    by_row = by_row.reshape(slots * MOST, 4 * units)
    pairs = jnp.dot(pick, by_row, preferred_element_type=jnp.float32)
    weighted = pairs * mix_weight.reshape(-1)[:, None]
    return weighted.astype(jnp.bfloat16).reshape(tok_rows, top, 4 * units)


def solution(mesh):
    fine = Mesh(mesh.devices.reshape(16, 2, 2, 4, 2), ("z", "xh", "core", "y", "xl"))
    tp = ("y", "xl")
    placed = (
        P(ED, tp),
        P(ED, None, tp),
        P(ED, None, tp),
        P(ED, None),
        P(),
        P(ED, None),
    )
    return jax.shard_map(
        body, mesh=fine, in_specs=placed, out_specs=P(ED, None, tp), check_vma=False
    )
```

time: 698 us -> 267 us (0.38)
  blocking collectives: 599 us -> 33.7 us
  waiting for transfers between devices: 53.9 us -> 161 us
  between operations: 0.08 us -> 13.5 us
  starting transfers between devices: 8.08 us -> 15.4 us
    all_to_all x1, blocking collectives: 572 us -> 33.7 us  [body(): lax.all_to_all(rows.reshape(slots, MOST, width), 'z', split_axis=0, conca...]
    all_gather x0 -> x1, waiting for transfers between devices: none -> 107 us  [body(): whole = lax.all_gather(arrived, PLANE, axis=0, tiled=False)]
    all_gather x1 -> x0, blocking collectives: 27.1 us -> none  [body(): token_rows = lax.all_gather(tokens, 'tp', axis=1, tiled=True)]
    transpose x0 -> x2, local copies, waits for them, and re-layouts: none -> 21.7 us  [the longest x1 20.8 us: body(): whole = whole.reshape(4, 8, slots, MOST, width).transpose(2, 0, 3, 1, 4)]
    broadcast_in_dim x2 -> x0, local copies, waits for them, and re-layouts: 8.88 us -> none  [the longest x1 8.07 us: body(): jnp.broadcast_to(slot_buffer.reshape(slot_total, 1, MOST, feature_width),...]
    all_to_all x1, starting transfers between devices: 8.08 us -> 15.4 us  [body(): lax.all_to_all(hidden.reshape(slots * 4, MOST, units), ED, split_axis=0,...]
  transfers between devices with their start and end apart: 1 -> 2, of which waited for: 1 -> 2; matrix products, arithmetic and copies ran while one was open for 0% -> 0% of each run, Pallas kernels for 0% -> 0%
where the time goes in v1:
time: 267 us; the launch traced here: 266 us
  waiting for transfers between devices  161 us (60%)
  blocking collectives  33.7 us (13%)
  local copies, waits for them, and re-layouts  28.3 us (11%)
  starting transfers between devices  15.4 us (6%)
  between operations  13.5 us (5%)
  matrix products  10.5 us (4%)
  other arithmetic  3.12 us (1%)
    all_gather x1, waiting for transfers between devices, body(): whole = lax.all_gather(arrived, PLANE, axis=0, tiled=False)  107 us
    all_to_all x1, waiting for transfers between devices, body(): lax.all_to_all(hidden.reshape(slots * 4, MOST, units), ED, split_axis=0,...  53.7 us
    all_to_all x1, blocking collectives, body(): lax.all_to_all(rows.reshape(slots, MOST, width), 'z', split_axis=0, conca...  33.7 us
    transpose x1, local copies, waits for them, and re-layouts, body(): whole = whole.reshape(4, 8, slots, MOST, width).transpose(2, 0, 3, 1, 4)  20.8 us
    all_to_all x1, starting transfers between devices, body(): lax.all_to_all(hidden.reshape(slots * 4, MOST, units), ED, split_axis=0,...  15.4 us
  transfers between devices with their start and end apart: 2, of which 2 were waited for; matrix products, arithmetic and copies ran while one was open for 0% of the time, Pallas kernels for 0%

profile of v1, /device:TPU:1, one launch (start us, length us, event | category | flops | bytes accessed | tf_op | source)
XLA Modules:
  0.0 265.6 jit_solution(9435692165482945716)
XLA Ops:
  6.5 0.0 copy-start
  6.5 0.0 all-gather.2.cloned.1.call-start
  6.5 0.9 copy.20
  7.4 0.1 eq.69
  7.6 0.1 eq.65
  7.7 0.8 convert_reduce_fusion
  8.5 0.6 reduce-window.6
  9.1 0.2 slice_reduce_fusion
  9.4 0.1 select_reduce_fusion
  9.5 0.1 reduce_sum.68
  9.6 0.1 reduce_sum.70
  9.8 0.1 reduce_sum.69
  9.9 1.3 fusion.10
  11.2 0.1 copy.22
  11.3 0.1 fusion.6
  11.4 1.2 convolution_convert_fusion
  12.6 33.7 %all_to_all.10 = bf16[16,32,384]{2,1,0:T(8,128)(2,1)} all-to-all(bf16[16,32,384]{2,1,0:T(8,128)(2,1)S(1)} %bitcast.41), channel_id=1, replica_groups=mesh['z'=16,'xh'=2,'core'=2,'y'=4,'xl'=2] {'z'}, dimensions={0} | all-to-all | bytes 786432 | tf_op jit(solution)/shard_map/all_to_all | solution.py:40
  46.3 0.0 all-gather.2.cloned.1.call-update
  46.3 107.5 %all-gather.2.cloned.1.call-done = bf16[32,512,384]{2,1,0:T(8,128)(2,1)} async-done(((bf16[1,512,384]{2,1,0:T(8,128)(2,1)}), bf16[32,512,384]{2,1,0:T(8,128)(2,1)}) %all-gather.2.cloned.1.call-update) | async-done | bytes 12582928 | tf_op jit(solution)/shard_map/all_gather | solution.py:43
  153.8 20.8 %copy.23 = bf16[16,4,32,8,384]{4,3,2,1,0:T(8,128)(2,1)S(1)} copy(bf16[16,4,32,8,384]{4,2,0,3,1:T(8,128)(2,1)} %bitcast.35) | data formatting | bytes 25165824 | tf_op jit(solution)/shard_map/transpose | solution.py:44
  174.6 3.2 %copy.26 = bf16[256,8,8,384]{3,1,2,0:T(8,128)(2,1)S(1)} copy(bf16[256,8,8,384]{3,2,1,0:T(8,128)(2,1)S(1)} %bitcast.34) | data formatting | bytes 25165824
  177.9 0.0 copy-done
  177.9 0.0 copy-start.2
  177.9 3.7 %fusion.2 = f32[2048,256]{1,0:T(8,128)S(1)} fusion(bf16[2048,3072]{1,0:T(8,128)(2,1)S(1)} %bitcast.36, bf16[1,3072,256]{2,1,0:T(8,128)(2,1)S(1)} %copy-done), kind=kOutput, calls=%fused_computation.3 | convolution fusion | flops 3221225472 | bytes 16252928 | tf_op jit(solution)/shard_map/dot_general | solution.py:46
  181.6 0.0 copy-done.2
  181.6 5.1 %fusion = bf16[2048,256]{1,0:T(8,128)(2,1)} fusion(bf16[2048,3072]{1,0:T(8,128)(2,1)S(1)} %bitcast.37, f32[2048,256]{1,0:T(8,128)S(1)} %fusion.2, bf16[1,3072,256]{2,1,0:T(8,128)(2,1)S(1)} %copy-done.2), kind=kOutput, calls=%fused_computation.1 | convolution fusion | flops 3224371200 | bytes 17301504 | tf_op jit(solution)/shard_map/dot_general | solution.py:47
  186.7 0.0 copy-start.1
  186.7 15.4 %all-to-all-start.1 = ((bf16[64,32,256]{2,1,0:T(8,128)(2,1)}), bf16[64,32,256]{2,1,0:T(8,128)(2,1)S(1)}, u32[]{:S(2)}, u32[]{:S(2)}) async-start(bf16[64,32,256]{2,1,0:T(8,128)(2,1)} %bitcast.42), calls=%async_computation.1 | async-start | bytes 2097152 | tf_op jit(solution)/shard_map/all_to_all | solution.py:50
  202.1 0.0 copy-done.1
  202.1 0.1 copy.25
  202.3 0.1 mul.62
  202.4 0.1 fusion.18
  202.5 53.7 %all-to-all-done.1 = bf16[64,32,256]{2,1,0:T(8,128)(2,1)S(1)} async-done(((bf16[64,32,256]{2,1,0:T(8,128)(2,1)}), bf16[64,32,256]{2,1,0:T(8,128)(2,1)S(1)}, u32[]{:S(2)}, u32[]{:S(2)}) %all-to-all-start.1) | async-done | bytes 1048608 | tf_op jit(solution)/shard_map/all_to_all | solution.py:50
  256.2 0.9 copy.24
  257.1 0.2 copy.27
  257.3 0.5 fusion.4
  257.8 1.0 reshape.89
  (3 shorter events, 0.0 us)
Async XLA Ops:
  6.5 171.3 %copy-start = (bf16[1,3072,256]{2,1,0:T(8,128)(2,1)S(1)}, bf16[1,3072,256]{2,1,0:T(8,128)(2,1)}, u32[]{:S(2)}) copy-start(bf16[1,3072,256]{2,1,0:T(8,128)(2,1)} %param.7) | copy-start | bytes 4718596
  6.5 147.3 %all-gather.2.cloned.1.call-start = ((), (), s32[]{:S(2)}) async-start(), calls=%async_computation.2 | async-start | bytes 12976128 | tf_op jit(solution)/shard_map/all_gather | solution.py:43
  177.9 3.7 %copy-start.2 = (bf16[1,3072,256]{2,1,0:T(8,128)(2,1)S(1)}, bf16[1,3072,256]{2,1,0:T(8,128)(2,1)}, u32[]{:S(2)}) copy-start(bf16[1,3072,256]{2,1,0:T(8,128)(2,1)} %param.8) | copy-start | bytes 4718596
  186.7 15.4 %copy-start.1 = (f32[128,2]{0,1:T(2,128)S(1)}, f32[128,2]{0,1:T(2,128)}, u32[]{:S(2)}) copy-start(f32[128,2]{0,1:T(2,128)} %param.11) | copy-start | bytes 3076
  186.7 69.5 %all-to-all-start.1 = ((bf16[64,32,256]{2,1,0:T(8,128)(2,1)}), bf16[64,32,256]{2,1,0:T(8,128)(2,1)S(1)}, u32[]{:S(2)}, u32[]{:S(2)}) async-start(bf16[64,32,256]{2,1,0:T(8,128)(2,1)} %bitcast.42), calls=%async_computation.1 | async-start | bytes 2097152 | tf_op jit(solution)/shard_map/all_to_all | solution.py:50
Sparse Core Ops, SparseCore 0:
  46.4 107.3 all-gather.1

commit v2 on v1

v2 whole, which is shorter than its diff:
```python
import jax
import jax.numpy as jnp
from jax import lax
from jax.experimental import pallas as pl
from jax.experimental.pallas import tpu as pltpu
from jax.sharding import Mesh, PartitionSpec as P

EXPERTS = 8
MOST = 32
SLOTS = 16
WIDTH = 384
UNITS = 256
ED = ("z", "xh", "core")
MESH = pl.DeviceIdType.MESH

PLAN = (
    ((0, 1), (-1, 8)),
    ((7, -6), (-7, 6)),
    ((5, -4), (-5, 4)),
    ((3, -2), (-3, 2)),
)
GROUPS = len(PLAN)
PER = 2
BLOCK = PER * MOST


def assign_slots(experts, placement):
    chosen_flat = experts.reshape(-1)
    expert_range = jnp.arange(EXPERTS, dtype=jnp.int32)
    holders = (placement[:, None] == expert_range[None, :]).astype(jnp.int32)
    replicas = jnp.sum(holders, axis=0)
    first_slot = jnp.sum((placement[:, None] < expert_range[None, :]).astype(jnp.int32), axis=0)
    chosen = (chosen_flat[:, None] == expert_range[None, :]).astype(jnp.int32)
    earlier = jnp.cumsum(chosen, axis=0) - chosen
    rank_index = jnp.sum(earlier * chosen, axis=1)
    replica_count = jnp.sum(chosen * replicas[None, :], axis=1)
    slot_start = jnp.sum(chosen * first_slot[None, :], axis=1)
    slot_index = slot_start + rank_index % replica_count
    position = rank_index // replica_count
    return (slot_index, position)


def kernel(
    rows, gate_hbm, up_hbm, pick, mix, out,
    full, gate_w, up_w, hidden, back,
    w_sem, z_send, z_recv, first_send, first_recv, second_send, second_recv,
    core_send, core_recv, back_send, back_recv,
):
    z, xh, core = lax.axis_index("z"), lax.axis_index("xh"), lax.axis_index("core")
    y, xl = lax.axis_index("y"), lax.axis_index("xl")
    x = xh * 2 + xl

    def x_at(step):
        other = lax.rem(x + step + 4, 4)
        return other // 2, lax.rem(other, 2)

    def y_at(step):
        return lax.rem(y + step + 4, 4)

    def z_at(step):
        return lax.rem(z + step + SLOTS, SLOTS)

    def x_device(step):
        other_h, other_l = x_at(step)
        return (z, other_h, core, y, other_l)

    def y_device(step):
        return (z, xh, core, y_at(step), xl)

    sibling = (z, xh, 1 - core, y, xl)

    def ed_device(dz, dh, dc):
        return (z_at(dz), 1 - xh if dh else xh, 1 - core if dc else core, y, xl)

    gate_copy = pltpu.make_async_copy(gate_hbm.at[0], gate_w, w_sem.at[0])
    up_copy = pltpu.make_async_copy(up_hbm.at[0], up_w, w_sem.at[1])
    gate_copy.start()
    up_copy.start()

    barrier = pltpu.get_barrier_semaphore()
    peers = 0
    for dz in range(SLOTS):
        for dh in range(2):
            for dc in range(2):
                if dz or dh or dc:
                    pl.semaphore_signal(
                        barrier, inc=1, device_id=ed_device(dz, dh, dc), device_id_type=MESH
                    )
                    peers += 1
    for step in (1, -1):
        pl.semaphore_signal(barrier, inc=1, device_id=x_device(step), device_id_type=MESH)
        pl.semaphore_signal(barrier, inc=1, device_id=y_device(step), device_id_type=MESH)
        peers += 2
    pl.semaphore_wait(barrier, peers)

    sends = []

    def remote(src, dst, send, recv, device):
        copy = pltpu.make_async_remote_copy(
            src_ref=src, dst_ref=dst, send_sem=send, recv_sem=recv,
            device_id=device, device_id_type=MESH,
        )
        copy.start()
        return copy

    def push(ref, send, recv, device):
        copy = remote(ref, ref, send, recv, device)
        sends.append(copy)

    def arrive(ref, recv):
        pltpu.make_async_copy(ref, ref, recv).wait()

    for g in range(GROUPS):
        for o in range(2):
            for j in range(PER):
                offset = PLAN[g][o][j]
                target = z_at(-offset)
                src = rows.at[pl.ds(pl.multiple_of(target * MOST, MOST), MOST)]
                dst = full.at[g, o, y, xl, xh, core, pl.ds(j * MOST, MOST)]
                if offset == 0:
                    pltpu.make_async_copy(src, dst, z_recv.at[g, o]).start()
                else:
                    remote(src, dst, z_send, z_recv.at[g, o], ed_device(-offset, 0, 0))

    def block(g, o, step):
        if o == 0:
            h, l = x_at(step)
            return full.at[g, o, y, l, h, core]
        return full.at[g, o, y_at(step), xl, xh, core]

    def half_block(g, o, step, half):
        part = pl.ds(half * (BLOCK // 2), BLOCK // 2)
        if o == 0:
            h, l = x_at(step)
            return full.at[g, o, y, l, h, core, part]
        return full.at[g, o, y_at(step), xl, xh, core, part]

    def slab(g, o, step):
        if o == 0:
            return full.at[g, o, y_at(step), :, :, core]
        h, l = x_at(step)
        return full.at[g, o, :, l, h, core]

    def half_slab(g, o, step, half):
        if o == 0:
            return full.at[g, o, y_at(step), half, :, core]
        h, l = x_at(step)
        return full.at[g, o, pl.ds(half * 2, 2), l, h, core]

    def first_device(o, step):
        return x_device(step) if o == 0 else y_device(step)

    def second_device(o, step):
        return y_device(step) if o == 0 else x_device(step)

    def to_core(g, o, ref):
        remote(ref, ref, core_send.at[g, o], core_recv.at[g, o], sibling)

    def stage0(g, o):
        arrive(block(g, o, 0), z_recv.at[g, o])
        for d, step in enumerate((1, -1)):
            push(block(g, o, 0), first_send.at[g, o, d], first_recv.at[g, o, d], first_device(o, step))

    def stage1(g, o):
        for d, step in enumerate((1, -1)):
            arrive(block(g, o, -step), first_recv.at[g, o, d])
            push(
                half_block(g, o, -step, d), first_send.at[g, o, 2 + d], first_recv.at[g, o, 2 + d],
                first_device(o, step),
            )

    def stage2(g, o):
        for d in range(2):
            arrive(half_block(g, o, 2, d), first_recv.at[g, o, 2 + d])
        for d, step in enumerate((1, -1)):
            push(slab(g, o, 0), second_send.at[g, o, d], second_recv.at[g, o, d], second_device(o, step))
        to_core(g, o, slab(g, o, 0))

    def stage3(g, o):
        for d, step in enumerate((1, -1)):
            arrive(slab(g, o, -step), second_recv.at[g, o, d])
            push(
                half_slab(g, o, -step, d), second_send.at[g, o, 2 + d], second_recv.at[g, o, 2 + d],
                second_device(o, step),
            )
            to_core(g, o, slab(g, o, -step))

    def stage4(g, o):
        for d in range(2):
            arrive(half_slab(g, o, 2, d), second_recv.at[g, o, 2 + d])
        to_core(g, o, slab(g, o, 2))

    def stage5(g, o):
        arrive(full.at[g, o, :, :, :, 1 - core], core_recv.at[g, o])
        left = jnp.concatenate(
            [full[g, o, t // 2, t % 2].reshape(4 * BLOCK, WIDTH) for t in range(8)], axis=1
        )
        gate_sum = jnp.dot(left, gate_w[...], preferred_element_type=jnp.float32)
        up_sum = jnp.dot(left, up_w[...], preferred_element_type=jnp.float32)
        units = gate_sum / (1.0 + jnp.exp(-gate_sum)) * up_sum
        hidden[g, o] = units.astype(jnp.bfloat16).reshape(2, 2, BLOCK, UNITS)
        for j in range(PER):
            offset = PLAN[g][o][j]
            for dh in range(2):
                for dc in range(2):
                    h = 1 - xh if dh else xh
                    c = 1 - core if dc else core
                    src = hidden.at[g, o, h, c, pl.ds(j * MOST, MOST)]
                    dst = back.at[xh * 2 + core, pl.ds(pl.multiple_of(z * MOST, MOST), MOST)]
                    if offset == 0 and not dh and not dc:
                        pltpu.make_async_copy(src, dst, back_recv).start()
                    else:
                        remote(src, dst, back_send.at[g, o], back_recv, ed_device(offset, dh, dc))

    stages = (stage0, stage1, stage2, stage3, stage4, stage5)
    for t in range(GROUPS + len(stages) - 1):
        if t == len(stages) - 1:
            gate_copy.wait()
            up_copy.wait()
        for s, stage in enumerate(stages):
            g = t - s
            if 0 <= g < GROUPS:
                for o in range(2):
                    stage(g, o)

    arrive(rows.at[pl.ds(0, (SLOTS - 1) * MOST)], z_send)
    for copy in sends:
        copy.wait_send()
    for g in range(GROUPS):
        for o in range(2):
            arrive(full.at[g, o, :, :, :, core], core_send.at[g, o])
            if 0 in PLAN[g][o]:
                arrive(hidden.at[g, o, 0], back_send.at[g, o])
                arrive(hidden.at[g, o, 1, 0], back_send.at[g, o])
                arrive(hidden.at[g, o, 1, 1, pl.ds(0, BLOCK - MOST)], back_send.at[g, o])
            else:
                arrive(hidden.at[g, o], back_send.at[g, o])
    arrive(back, back_recv)
    for g in range(4):
        pairs = jnp.dot(pick[...], back[g], preferred_element_type=jnp.float32)
        out[:, g * UNITS:(g + 1) * UNITS] = (pairs * mix[...]).astype(jnp.bfloat16)


def body(tokens, gate_weight, up_weight, experts, placement, mix_weight):
    tok_rows, width = tokens.shape
    top = experts.shape[1]
    slots = placement.shape[0]
    slot_index, position = assign_slots(experts, placement)
    place = slot_index * MOST + position
    spots = jnp.arange(slots * MOST, dtype=jnp.int32)
    pick = (place[:, None] == spots[None, :]).astype(jnp.bfloat16)
    spread = jnp.sum(pick.reshape(tok_rows, top, slots * MOST), axis=1)
    rows = lax.dot_general(
        spread, tokens, (((0,), (0,)), ((), ())), preferred_element_type=jnp.float32
    ).astype(jnp.bfloat16)
    vmem = pl.BlockSpec(memory_space=pltpu.VMEM)
    anywhere = pl.BlockSpec(memory_space=pl.ANY)
    dma = pltpu.SemaphoreType.DMA
    feature_count = gate_weight.shape[1]
    weighted = pl.pallas_call(
        kernel,
        out_shape=jax.ShapeDtypeStruct((tok_rows * top, 4 * UNITS), jnp.bfloat16),
        in_specs=[vmem, anywhere, anywhere, vmem, vmem],
        out_specs=vmem,
        scratch_shapes=[
            pltpu.VMEM((GROUPS, 2, 4, 2, 2, 2, BLOCK, WIDTH), jnp.bfloat16),
            pltpu.VMEM((feature_count, UNITS), jnp.bfloat16),
            pltpu.VMEM((feature_count, UNITS), jnp.bfloat16),
            pltpu.VMEM((GROUPS, 2, 2, 2, BLOCK, UNITS), jnp.bfloat16),
            pltpu.VMEM((4, slots * MOST, UNITS), jnp.bfloat16),
            dma((2,)),
            dma,
            dma((GROUPS, 2)),
            dma((GROUPS, 2, 4)),
            dma((GROUPS, 2, 4)),
            dma((GROUPS, 2, 4)),
            dma((GROUPS, 2, 4)),
            dma((GROUPS, 2)),
            dma((GROUPS, 2)),
            dma((GROUPS, 2)),
            dma,
        ],
        compiler_params=pltpu.CompilerParams(
            collective_id=0, has_side_effects=True, vmem_limit_bytes=48 * 1024 * 1024
        ),
        cost_estimate=pl.CostEstimate(
            flops=2 * 2048 * 3072 * 512, bytes_accessed=4 << 20, transcendentals=2048 * 256
        ),
    )(rows, gate_weight, up_weight, pick, mix_weight.reshape(-1)[:, None])
    return weighted.reshape(tok_rows, top, 4 * UNITS)


def solution(mesh):
    fine = Mesh(mesh.devices.reshape(16, 2, 2, 4, 2), ("z", "xh", "core", "y", "xl"))
    tp = ("y", "xl")
    placed = (
        P(ED, tp),
        P(ED, None, tp),
        P(ED, None, tp),
        P(ED, None),
        P(),
        P(ED, None),
    )
    return jax.shard_map(
        body, mesh=fine, in_specs=placed, out_specs=P(ED, None, tp), check_vma=False
    )
```

time: 267 us -> 119 us (0.45)
  waiting for transfers between devices: 161 us -> 0 us
  Pallas kernels: 0 us -> 110 us
  blocking collectives: 33.7 us -> 0 us
  local copies, waits for them, and re-layouts: 28.3 us -> 5.04 us
  starting transfers between devices: 15.4 us -> 0 us
  between operations: 13.5 us -> 0.12 us
  matrix products: 10.5 us -> 0.28 us
    pallas_call x0 -> x1, Pallas kernels: none -> 110 us  [body(): pl.pallas_call(kernel, out_shape=jax.ShapeDtypeStruct((tok_rows * top, 4...]
    all_gather x1 -> x0, waiting for transfers between devices: 107 us -> none  [body(): whole = lax.all_gather(arrived, PLANE, axis=0, tiled=False)]
    all_to_all x1 -> x0, waiting for transfers between devices: 53.7 us -> none  [body(): lax.all_to_all(hidden.reshape(slots * 4, MOST, units), ED, split_axis=0,...]
    all_to_all x1 -> x0, blocking collectives: 33.7 us -> none  [body(): lax.all_to_all(rows.reshape(slots, MOST, width), 'z', split_axis=0, conca...]
    transpose x2 -> x0, local copies, waits for them, and re-layouts: 21.7 us -> none  [the longest x1 20.8 us: body(): whole = whole.reshape(4, 8, slots, MOST, width).transpose(2, 0, 3, 1, 4)]
    all_to_all x1 -> x0, starting transfers between devices: 15.4 us -> none  [body(): lax.all_to_all(hidden.reshape(slots * 4, MOST, units), ED, split_axis=0,...]
    dot_general x3 -> x0, matrix products: 9.28 us -> none  [the longest x1 5.11 us: body(): up_sum = jnp.dot(whole, up_weight[0], preferred_element_type=jnp.float32)]
  transfers between devices with their start and end apart: 2 -> 0, of which waited for: 2 -> 0; matrix products, arithmetic and copies ran while one was open for 0% -> 0% of each run, Pallas kernels for 0% -> 0%
where the time goes in v2:
time: 119 us
  Pallas kernels  110 us (92%)
  local copies, waits for them, and re-layouts  5.04 us (4%)
  other arithmetic  3.33 us (3%)
    pallas_call x1, Pallas kernels, body(): pl.pallas_call(kernel, out_shape=jax.ShapeDtypeStruct((tok_rows * top, 4...  110 us
    unnamed x8, local copies, waits for them, and re-layouts  3.01 us

profile of v2, /device:TPU:1, one launch (start us, length us, event | category | flops | bytes accessed | tf_op | source)
XLA Modules:
  0.0 119.2 jit_solution(6924656693472839110)
XLA Ops:
  0.0 0.0 copy-start
  0.0 0.0 copy-start.1
  0.0 0.9 convert_reduce_fusion
  0.9 0.8 copy.12
  1.7 0.1 eq.69
  1.9 0.1 eq.65
  2.0 0.6 reduce-window.6
  2.6 0.2 slice_reduce_fusion
  2.9 0.1 select_reduce_fusion
  3.0 0.1 fusion.13
  3.1 0.1 reduce_sum.65
  3.2 0.1 reduce_sum.70
  3.4 0.1 reduce_sum.67
  3.5 1.3 %fusion.5 = s32[128,2]{1,0:T(8,128)S(1)} fusion(s32[128,2]{1,0:T(8,128)S(1)} %reduce_sum.65, s32[128,2]{1,0:T(8,128)S(1)} %reduce_sum.67, s32[128,2]{1,0:T(8,128)S(1)} %reduce_sum.70), kind=kLoop, calls=%fused_computation.11 | loop fusion | flops 5632 | bytes 4096 | tf_op jit(solution)/shard_map/add | solution.py:249
  4.9 0.1 copy.14
  4.9 0.8 copy.15
  5.7 0.1 broadcast_in_dim_reshape.5.mix
  5.8 0.1 fusion.2
  5.9 0.1 fusion.1.pick
  6.0 0.0 copy-done
  6.1 0.3 convolution_convert_fusion.rows
  6.3 0.0 copy-done.1
  6.3 0.0 copy-start.2
  6.4 1.4 %copy-done.2 = bf16[1,3072,256]{2,1,0:T(8,128)(2,1)S(1)} copy-done((bf16[1,3072,256]{2,1,0:T(8,128)(2,1)S(1)}, bf16[1,3072,256]{2,1,0:T(8,128)(2,1)}, u32[]{:S(2)}) %copy-start.2) | copy-done | bytes 1572888
  7.8 110.5 %shard_map.64 = bf16[256,1024]{1,0:T(8,128)(2,1)S(1)} custom-call(bf16[512,384]{1,0:T(8,128)(2,1)S(1)} %convolution_convert_fusion.rows, bf16[1,3072,256]{2,1,0:T(8,128)(2,1)S(1)} %copy-done.1, bf16[1,3072,256]{2,1,0:T(8,128)(2,1)S(1)} %copy-done.2, bf16[256,512]{1,0:T(8,128)(2,1)S(1)} %fusion.1.pick, f32[256,1]{1,0:T(8,128)S(1)} %broadcast_in_dim_reshape.5.mix), custom_call_target="tpu_custom_call" | custom-call | flops 6442450944 | bytes 4194304 | tf_op jit(solution)/shard_map/pallas_call | solution.py:260
  118.2 1.0 reshape.64
  (3 shorter events, 0.0 us)
Async XLA Ops:
  0.0 6.0 %copy-start = (bf16[128,384]{1,0:T(8,128)(2,1)S(1)}, bf16[128,384]{1,0:T(8,128)(2,1)}, u32[]{:S(2)}) copy-start(bf16[128,384]{1,0:T(8,128)(2,1)} %param.6) | copy-start | bytes 294916
  0.0 6.3 %copy-start.1 = (bf16[1,3072,256]{2,1,0:T(8,128)(2,1)S(1)}, bf16[1,3072,256]{2,1,0:T(8,128)(2,1)}, u32[]{:S(2)}) copy-start(bf16[1,3072,256]{2,1,0:T(8,128)(2,1)} %gate_hbm.1) | copy-start | bytes 4718596
  6.3 1.4 %copy-start.2 = (bf16[1,3072,256]{2,1,0:T(8,128)(2,1)S(1)}, bf16[1,3072,256]{2,1,0:T(8,128)(2,1)}, u32[]{:S(2)}) copy-start(bf16[1,3072,256]{2,1,0:T(8,128)(2,1)} %up_hbm.1) | copy-start | bytes 4718596

commit v3 on v2

v3 whole, which is shorter than its diff:
```python
import jax
import jax.numpy as jnp
from jax import lax
from jax.experimental import pallas as pl
from jax.experimental.pallas import tpu as pltpu
from jax.sharding import Mesh, PartitionSpec as P

MOST = 32
SLOTS = 16
WIDTH = 384
UNITS = 256
TOK = 128
EXPERT_ROWS = 16
ED = ("z", "xh", "core")
MESH = pl.DeviceIdType.MESH

PLAN = (
    ((7,), (-7,)),
    ((6,), (-6,)),
    ((8, -5), (5, 4)),
    ((-4, 3), (-3, 2)),
    ((-2, 1), (-1, 0)),
)
GROUPS = len(PLAN)
PER = tuple(len(orders[0]) for orders in PLAN)
START = tuple(sum(2 * per * MOST for per in PER[:g]) for g in range(GROUPS))
LAG = 1.5
WAVE = 2
ORDER = (2, 3, 4, 1, 0, 5)
LAST = len(ORDER) - 1
SCHEDULE = sorted(
    ((s, g) for g in range(GROUPS) for s in range(LAST + 1)),
    key=lambda item: (item[0] + LAG * item[1], ORDER.index(item[0])),
)


def place_rows(experts, placement):
    named = lax.broadcasted_iota(jnp.int32, (EXPERT_ROWS, TOK), 0)
    chosen = [experts[k:k + 1, :] == named for k in range(2)]
    counts = (chosen[0].astype(jnp.float32) + chosen[1].astype(jnp.float32)).astype(jnp.bfloat16)
    before = lax.broadcasted_iota(jnp.int32, (TOK, TOK), 0) < lax.broadcasted_iota(jnp.int32, (TOK, TOK), 1)
    earlier = jnp.dot(counts, before.astype(jnp.bfloat16), preferred_element_type=jnp.float32)
    expert_of_slot = lax.broadcasted_iota(jnp.int32, (EXPERT_ROWS, SLOTS), 0)
    replicas = jnp.sum((placement == expert_of_slot).astype(jnp.float32), axis=1, keepdims=True)
    first = jnp.sum((placement < expert_of_slot).astype(jnp.float32), axis=1, keepdims=True)
    found = []
    for k in range(2):
        own = chosen[k].astype(jnp.float32)
        rank = jnp.sum(own * earlier, axis=0, keepdims=True)
        replica_count = jnp.sum(own * replicas, axis=0, keepdims=True)
        start = jnp.sum(own * first, axis=0, keepdims=True)
        position = jnp.floor((rank + 0.5) / replica_count)
        found.append((start + rank - position * replica_count, position))
    return found


def spread_rows(found):
    spot = lax.broadcasted_iota(jnp.int32, (SLOTS * MOST, TOK), 0).astype(jnp.float32)
    hits = [(slot * MOST + position == spot).astype(jnp.float32) for slot, position in found]
    return (hits[0] + hits[1]).astype(jnp.bfloat16)


def pick_rows(found, mix):
    lines = [found[0][0], found[1][0], found[0][1], found[1][1]]
    rest = mix
    for part in range(3):
        piece = rest.astype(jnp.bfloat16).astype(jnp.float32)
        rest = rest - piece
        lines += [piece[0:1, :], piece[1:2, :]]
    table = jnp.concatenate(lines + [jnp.zeros((EXPERT_ROWS - len(lines), TOK), jnp.float32)], axis=0)
    pair = lax.broadcasted_iota(jnp.int32, (2 * TOK, TOK), 0)
    token = lax.broadcasted_iota(jnp.int32, (2 * TOK, TOK), 1)
    mine = jnp.logical_or(pair == 2 * token, pair == 2 * token + 1)
    per_pair = lax.dot_general(
        mine.astype(jnp.bfloat16), table.astype(jnp.bfloat16), (((1,), (1,)), ((), ())),
        preferred_element_type=jnp.float32,
    )
    second = jnp.bitwise_and(lax.broadcasted_iota(jnp.int32, (2 * TOK, 1), 0), 1) == 1
    values = [jnp.where(second, per_pair[:, 2 * v + 1:2 * v + 2], per_pair[:, 2 * v:2 * v + 1]) for v in range(5)]
    spot = lax.broadcasted_iota(jnp.int32, (2 * TOK, SLOTS * MOST), 1).astype(jnp.float32)
    pick = (values[0] * MOST + values[1] == spot).astype(jnp.float32).astype(jnp.bfloat16)
    return pick, (values[2] + values[3]) + values[4]


def kernel(
    tokens_hbm, gate_hbm, up_hbm, experts_hbm, placement_hbm, mix_hbm, out,
    tokens, experts, placement, mix, rows, pick, scale, full, gate_w, up_w, hidden, back,
    w_sem, z_send, z_recv, first_send, first_recv, second_send, second_recv,
    core_send, core_recv, back_send, back_recv,
):
    z, xh, core = lax.axis_index("z"), lax.axis_index("xh"), lax.axis_index("core")
    y, xl = lax.axis_index("y"), lax.axis_index("xl")
    x = xh * 2 + xl

    def x_at(step):
        other = lax.rem(x + step + 4, 4)
        return other // 2, lax.rem(other, 2)

    def y_at(step):
        return lax.rem(y + step + 4, 4)

    def z_at(step):
        return lax.rem(z + step + SLOTS, SLOTS)

    def x_device(step):
        other_h, other_l = x_at(step)
        return (z, other_h, core, y, other_l)

    def y_device(step):
        return (z, xh, core, y_at(step), xl)

    sibling = (z, xh, 1 - core, y, xl)

    def ed_device(dz, dh, dc):
        return (z_at(dz), 1 - xh if dh else xh, 1 - core if dc else core, y, xl)

    barrier = pltpu.get_barrier_semaphore()
    peers = [ed_device(dz, 0, 0) for dz in range(1, SLOTS)] + [sibling]
    peers += [device(step) for device in (x_device, y_device) for step in (1, -1)]
    for peer in peers:
        pl.semaphore_signal(barrier, inc=1, device_id=peer, device_id_type=MESH)

    loads = [
        pltpu.make_async_copy(src, dst, w_sem.at[i])
        for i, (src, dst) in enumerate((
            (experts_hbm, experts), (placement_hbm, placement), (tokens_hbm, tokens),
            (mix_hbm, mix), (gate_hbm.at[0], gate_w), (up_hbm.at[0], up_w),
        ))
    ]
    for load in loads:
        load.start()
    loads[0].wait()
    loads[1].wait()
    found = place_rows(experts[...], placement[...])
    loads[2].wait()
    rows[...] = jnp.dot(
        spread_rows(found), tokens[...], preferred_element_type=jnp.float32
    ).astype(jnp.bfloat16)

    pl.semaphore_wait(barrier, len(peers))

    sends = []

    def remote(src, dst, send, recv, device):
        copy = pltpu.make_async_remote_copy(
            src_ref=src, dst_ref=dst, send_sem=send, recv_sem=recv,
            device_id=device, device_id_type=MESH,
        )
        copy.start()
        return copy

    def push(ref, send, recv, device):
        copy = remote(ref, ref, send, recv, device)
        sends.append(copy)

    def arrive(ref, recv):
        pltpu.make_async_copy(ref, ref, recv).wait()

    def send_rows(g):
        for o in range(2):
            for j, offset in enumerate(PLAN[g][o]):
                src = rows.at[pl.ds(pl.multiple_of(z_at(-offset) * MOST, MOST), MOST)]
                dst = full.at[y, xl, xh, core, pl.ds(begin(g, o) + j * MOST, MOST)]
                if offset == 0:
                    pltpu.make_async_copy(src, dst, z_recv.at[g, o]).start()
                else:
                    remote(src, dst, z_send, z_recv.at[g, o], ed_device(-offset, 0, 0))

    def begin(g, o):
        return START[g] + o * PER[g] * MOST

    def span(g, o):
        return pl.ds(begin(g, o), PER[g] * MOST)

    def block(g, o, step):
        if o == 0:
            h, l = x_at(step)
            return full.at[y, l, h, core, span(g, o)]
        return full.at[y_at(step), xl, xh, core, span(g, o)]

    def half_block(g, o, step, half):
        size = PER[g] * MOST // 2
        part = pl.ds(begin(g, o) + half * size, size)
        if o == 0:
            h, l = x_at(step)
            return full.at[y, l, h, core, part]
        return full.at[y_at(step), xl, xh, core, part]

    def slab(g, o, step):
        if o == 0:
            return full.at[y_at(step), :, :, core, span(g, o)]
        h, l = x_at(step)
        return full.at[:, l, h, core, span(g, o)]

    def half_slab(g, o, step, half):
        if o == 0:
            return full.at[y_at(step), half, :, core, span(g, o)]
        h, l = x_at(step)
        return full.at[pl.ds(half * 2, 2), l, h, core, span(g, o)]

    def first_device(o, step):
        return x_device(step) if o == 0 else y_device(step)

    def second_device(o, step):
        return y_device(step) if o == 0 else x_device(step)

    def to_core(g, o, ref):
        remote(ref, ref, core_send.at[g, o], core_recv.at[g, o], sibling)

    def stage0(g, o):
        arrive(block(g, o, 0), z_recv.at[g, o])
        for d, step in enumerate((1, -1)):
            push(block(g, o, 0), first_send.at[g, o, d], first_recv.at[g, o, d], first_device(o, step))

    def stage1(g, o):
        for d, step in enumerate((1, -1)):
            arrive(block(g, o, -step), first_recv.at[g, o, d])
            push(
                half_block(g, o, -step, d), first_send.at[g, o, 2 + d], first_recv.at[g, o, 2 + d],
                first_device(o, step),
            )

    def stage2(g, o):
        for d in range(2):
            arrive(half_block(g, o, 2, d), first_recv.at[g, o, 2 + d])
        for d, step in enumerate((1, -1)):
            push(slab(g, o, 0), second_send.at[g, o, d], second_recv.at[g, o, d], second_device(o, step))
        to_core(g, o, slab(g, o, 0))

    def stage3(g, o):
        for d, step in enumerate((1, -1)):
            arrive(slab(g, o, -step), second_recv.at[g, o, d])
            push(
                half_slab(g, o, -step, d), second_send.at[g, o, 2 + d], second_recv.at[g, o, 2 + d],
                second_device(o, step),
            )
            to_core(g, o, slab(g, o, -step))

    def stage4(g, o):
        for d in range(2):
            arrive(half_slab(g, o, 2, d), second_recv.at[g, o, 2 + d])
        to_core(g, o, slab(g, o, 2))

    def stage5(g):
        for o in range(2):
            arrive(full.at[:, :, :, 1 - core, span(g, o)], core_recv.at[g, o])
        count = 2 * PER[g] * MOST
        both = pl.ds(START[g], count)
        left = jnp.concatenate(
            [full[t // 2, t % 2, :, :, both, :].reshape(4 * count, WIDTH) for t in range(8)], axis=1
        )
        gate_sum = jnp.dot(left, gate_w[...], preferred_element_type=jnp.float32)
        up_sum = jnp.dot(left, up_w[...], preferred_element_type=jnp.float32)
        units = gate_sum / (1.0 + jnp.exp(-gate_sum)) * up_sum
        hidden[:, :, both, :] = units.astype(jnp.bfloat16).reshape(2, 2, count, UNITS)
        for o in range(2):
            for j, offset in enumerate(PLAN[g][o]):
                for dh in range(2):
                    for dc in range(2):
                        h = 1 - xh if dh else xh
                        c = 1 - core if dc else core
                        src = hidden.at[h, c, pl.ds(begin(g, o) + j * MOST, MOST)]
                        dst = back.at[xh * 2 + core, pl.ds(pl.multiple_of(z * MOST, MOST), MOST)]
                        if offset == 0 and not dh and not dc:
                            pltpu.make_async_copy(src, dst, back_recv).start()
                        else:
                            remote(src, dst, back_send.at[g], back_recv, ed_device(offset, dh, dc))

    for g in range(WAVE):
        send_rows(g)
    loads[3].wait()
    found_pick, found_scale = pick_rows(found, mix[...])
    pick[...] = found_pick
    scale[...] = found_scale
    stages = (stage0, stage1, stage2, stage3, stage4)
    for s, g in SCHEDULE:
        if s == LAST:
            if g == 0:
                loads[4].wait()
                loads[5].wait()
            stage5(g)
            continue
        for o in range(2):
            stages[s](g, o)
        if s == 0 and g + WAVE < GROUPS:
            send_rows(g + WAVE)

    arrive(rows.at[pl.ds(0, (SLOTS - 1) * MOST)], z_send)
    for copy in sends:
        copy.wait_send()
    for g in range(GROUPS):
        for o in range(2):
            arrive(full.at[:, :, :, core, span(g, o)], core_send.at[g, o])
        count = 2 * PER[g] * MOST
        if 0 in PLAN[g][0] + PLAN[g][1]:
            arrive(hidden.at[0, :, pl.ds(START[g], count)], back_send.at[g])
            arrive(hidden.at[1, 0, pl.ds(START[g], count)], back_send.at[g])
            arrive(hidden.at[1, 1, pl.ds(START[g], count - MOST)], back_send.at[g])
        else:
            arrive(hidden.at[:, :, pl.ds(START[g], count)], back_send.at[g])
    arrive(back, back_recv)
    for g in range(4):
        pairs = jnp.dot(pick[...], back[g], preferred_element_type=jnp.float32)
        out[:, g * UNITS:(g + 1) * UNITS] = (pairs * scale[...]).astype(jnp.bfloat16)


def body(tokens, gate_weight, up_weight, experts, placement, mix_weight):
    tok_rows, width = tokens.shape
    top = experts.shape[1]
    slots = placement.shape[0]
    vmem = pl.BlockSpec(memory_space=pltpu.VMEM)
    hbm = pl.BlockSpec(memory_space=pltpu.HBM)
    dma = pltpu.SemaphoreType.DMA
    feature_count = gate_weight.shape[1]
    weighted = pl.pallas_call(
        kernel,
        out_shape=jax.ShapeDtypeStruct((tok_rows * top, 4 * UNITS), jnp.bfloat16),
        in_specs=[hbm] * 6,
        out_specs=vmem,
        scratch_shapes=[
            pltpu.VMEM((tok_rows, width), jnp.bfloat16),
            pltpu.VMEM((top, tok_rows), jnp.int32),
            pltpu.VMEM((1, slots), jnp.int32),
            pltpu.VMEM((top, tok_rows), jnp.float32),
            pltpu.VMEM((slots * MOST, width), jnp.bfloat16),
            pltpu.VMEM((tok_rows * top, slots * MOST), jnp.bfloat16),
            pltpu.VMEM((tok_rows * top, 1), jnp.float32),
            pltpu.VMEM((4, 2, 2, 2, slots * MOST, width), jnp.bfloat16),
            pltpu.VMEM((feature_count, UNITS), jnp.bfloat16),
            pltpu.VMEM((feature_count, UNITS), jnp.bfloat16),
            pltpu.VMEM((2, 2, slots * MOST, UNITS), jnp.bfloat16),
            pltpu.VMEM((4, slots * MOST, UNITS), jnp.bfloat16),
            dma((6,)),
            dma,
            dma((GROUPS, 2)),
            dma((GROUPS, 2, 4)),
            dma((GROUPS, 2, 4)),
            dma((GROUPS, 2, 4)),
            dma((GROUPS, 2, 4)),
            dma((GROUPS, 2)),
            dma((GROUPS, 2)),
            dma((GROUPS,)),
            dma,
        ],
        compiler_params=pltpu.CompilerParams(
            collective_id=0, has_side_effects=True, vmem_limit_bytes=60 * 1024 * 1024
        ),
        cost_estimate=pl.CostEstimate(
            flops=2 * 2048 * 3072 * 512, bytes_accessed=4 << 20, transcendentals=2048 * 256
        ),
    )(tokens, gate_weight, up_weight, experts.T, placement.reshape(1, slots), mix_weight.T)
    return weighted.reshape(tok_rows, top, 4 * UNITS)


def solution(mesh):
    fine = Mesh(mesh.devices.reshape(16, 2, 2, 4, 2), ("z", "xh", "core", "y", "xl"))
    tp = ("y", "xl")
    placed = (
        P(ED, tp),
        P(ED, None, tp),
        P(ED, None, tp),
        P(ED, None),
        P(),
        P(ED, None),
    )
    return jax.shard_map(
        body, mesh=fine, in_specs=placed, out_specs=P(ED, None, tp), check_vma=False
    )
```

time: 119 us -> 100 us (0.84)
  Pallas kernels: 110 us -> 97.8 us
  other arithmetic: 3.33 us -> 0 us
  local copies, waits for them, and re-layouts: 5.04 us -> 2.03 us
    pallas_call x1, Pallas kernels: 110 us -> 97.8 us  [body(): pl.pallas_call(kernel, out_shape=jax.ShapeDtypeStruct((tok_rows * top, 4...]
    unnamed x8 -> x0, local copies, waits for them, and re-layouts: 3.01 us -> none
    add x2 -> x0, other arithmetic: 1.46 us -> none  [body(): place = slot_index * MOST + position]
where the time goes in v3:
time: 100 us; the launch traced here: 99.8 us
  Pallas kernels  97.8 us (98%)
  local copies, waits for them, and re-layouts  2.03 us (2%)
    pallas_call x1, Pallas kernels, body(): pl.pallas_call(kernel, out_shape=jax.ShapeDtypeStruct((tok_rows * top, 4...  97.8 us
    reshape x1, local copies, waits for them, and re-layouts, body(): return weighted.reshape(tok_rows, top, 4 * UNITS)  2.03 us

profile of v3, /device:TPU:1, one launch (start us, length us, event | category | flops | bytes accessed | tf_op | source)
XLA Modules:
  0.0 99.8 jit_solution(12174721793099771149)
XLA Ops:
  0.0 97.8 %shard_map.64 = bf16[256,1024]{1,0:T(8,128)(2,1)} custom-call(bf16[128,384]{1,0:T(8,128)(2,1)} %tokens_hbm.1, bf16[1,3072,256]{2,1,0:T(8,128)(2,1)} %gate_hbm.1, bf16[1,3072,256]{2,1,0:T(8,128)(2,1)} %up_hbm.1, s32[2,128]{1,0:T(2,128)} %bitcast.3, s32[1,16]{1,0:T(1,128)} %bitcast.5, f32[2,128]{1,0:T(2,128)} %bitcast.4), custom_call_target="tpu_custom_call" | custom-call | flops 6442450944 | bytes 4194304 | tf_op jit(solution)/shard_map/pallas_call | solution.py:315
  97.8 2.0 %reshape.7 = bf16[128,2,1024]{2,1,0:T(2,128)(2,1)} reshape(bf16[256,1024]{1,0:T(8,128)(2,1)} %shard_map.64) | data formatting | bytes 1048576 | tf_op jit(solution)/shard_map/reshape | solution.py:352

commit v4 on v3

--- a/solution.py
+++ b/solution.py
@@ -15,22 +15,28 @@
 MESH = pl.DeviceIdType.MESH
 
 PLAN = (
+    ((5,), (-5,)),
     ((7,), (-7,)),
     ((6,), (-6,)),
-    ((8, -5), (5, 4)),
-    ((-4, 3), (-3, 2)),
-    ((-2, 1), (-1, 0)),
+    ((8, -4), (4, 3)),
+    ((-3, 2), (-2, 0)),
+    ((1,), (-1,)),
 )
 GROUPS = len(PLAN)
 PER = tuple(len(orders[0]) for orders in PLAN)
+DIRECT = 6
 START = tuple(sum(2 * per * MOST for per in PER[:g]) for g in range(GROUPS))
-LAG = 1.5
-WAVE = 2
-ORDER = (2, 3, 4, 1, 0, 5)
-LAST = len(ORDER) - 1
-SCHEDULE = sorted(
-    ((s, g) for g in range(GROUPS) for s in range(LAST + 1)),
-    key=lambda item: (item[0] + LAG * item[1], ORDER.index(item[0])),
+ROWS, RETURN = -1, 5
+SCHEDULE = (
+    (-1, 2, 0), (-1, 1, 0), (-1, 3, 0), (0, 2, 1), (0, 2, 0), (-1, 5, 0), (0, 1, 0), (0, 1, 1),
+    (1, 2, 1), (2, 2, 1), (1, 2, 0), (2, 2, 0), (-1, 0, 0), (0, 3, 0), (1, 1, 1), (1, 1, 0),
+    (-1, 4, 0), (0, 3, 1), (2, 1, 1), (0, 5, 1), (2, 1, 0), (3, 2, 1), (4, 2, 1), (0, 5, 0),
+    (3, 2, 0), (4, 2, 0), (1, 3, 1), (1, 3, 0), (2, 3, 0), (2, 3, 1), (5, 2, 0), (0, 0, 0),
+    (3, 1, 0), (3, 1, 1), (1, 5, 1), (4, 1, 1), (4, 1, 0), (0, 4, 0), (1, 5, 0), (0, 0, 1),
+    (2, 5, 1), (0, 4, 1), (5, 1, 0), (3, 3, 1), (2, 5, 0), (3, 3, 0), (4, 3, 1), (4, 3, 0),
+    (1, 0, 1), (2, 0, 1), (1, 0, 0), (1, 4, 1), (1, 4, 0), (2, 0, 0), (2, 4, 1), (2, 4, 0),
+    (5, 3, 0), (3, 5, 0), (3, 5, 1), (4, 5, 1), (3, 0, 1), (3, 0, 0), (4, 0, 0), (4, 0, 1),
+    (4, 5, 0), (3, 4, 0), (5, 0, 0), (3, 4, 1), (4, 4, 0), (4, 4, 1), (5, 5, 0), (5, 4, 0),
 )
 
 
@@ -116,7 +122,7 @@
 
     barrier = pltpu.get_barrier_semaphore()
     peers = [ed_device(dz, 0, 0) for dz in range(1, SLOTS)] + [sibling]
-    peers += [device(step) for device in (x_device, y_device) for step in (1, -1)]
+    peers += [device(step) for device in (x_device, y_device) for step in (1, -1, 2)]
     for peer in peers:
         pl.semaphore_signal(barrier, inc=1, device_id=peer, device_id_type=MESH)
 
@@ -207,38 +213,49 @@
     def to_core(g, o, ref):
         remote(ref, ref, core_send.at[g, o], core_recv.at[g, o], sibling)
 
+    def ways(g):
+        return (1, -1, 2) if g < DIRECT else (1, -1)
+
     def stage0(g, o):
         arrive(block(g, o, 0), z_recv.at[g, o])
-        for d, step in enumerate((1, -1)):
+        for d, step in enumerate(ways(g)):
             push(block(g, o, 0), first_send.at[g, o, d], first_recv.at[g, o, d], first_device(o, step))
 
     def stage1(g, o):
         for d, step in enumerate((1, -1)):
             arrive(block(g, o, -step), first_recv.at[g, o, d])
-            push(
-                half_block(g, o, -step, d), first_send.at[g, o, 2 + d], first_recv.at[g, o, 2 + d],
-                first_device(o, step),
-            )
+            if g >= DIRECT:
+                push(
+                    half_block(g, o, -step, d), first_send.at[g, o, 2 + d], first_recv.at[g, o, 2 + d],
+                    first_device(o, step),
+                )
 
     def stage2(g, o):
-        for d in range(2):
-            arrive(half_block(g, o, 2, d), first_recv.at[g, o, 2 + d])
-        for d, step in enumerate((1, -1)):
+        if g < DIRECT:
+            arrive(block(g, o, 2), first_recv.at[g, o, 2])
+        else:
+            for d in range(2):
+                arrive(half_block(g, o, 2, d), first_recv.at[g, o, 2 + d])
+        for d, step in enumerate(ways(g)):
             push(slab(g, o, 0), second_send.at[g, o, d], second_recv.at[g, o, d], second_device(o, step))
         to_core(g, o, slab(g, o, 0))
 
     def stage3(g, o):
         for d, step in enumerate((1, -1)):
             arrive(slab(g, o, -step), second_recv.at[g, o, d])
-            push(
-                half_slab(g, o, -step, d), second_send.at[g, o, 2 + d], second_recv.at[g, o, 2 + d],
-                second_device(o, step),
-            )
+            if g >= DIRECT:
+                push(
+                    half_slab(g, o, -step, d), second_send.at[g, o, 2 + d], second_recv.at[g, o, 2 + d],
+                    second_device(o, step),
+                )
             to_core(g, o, slab(g, o, -step))
 
     def stage4(g, o):
-        for d in range(2):
-            arrive(half_slab(g, o, 2, d), second_recv.at[g, o, 2 + d])
+        if g < DIRECT:
+            arrive(slab(g, o, 2), second_recv.at[g, o, 2])
+        else:
+            for d in range(2):
+                arrive(half_slab(g, o, 2, d), second_recv.at[g, o, 2 + d])
         to_core(g, o, slab(g, o, 2))
 
     def stage5(g):
@@ -266,24 +283,26 @@
                         else:
                             remote(src, dst, back_send.at[g], back_recv, ed_device(offset, dh, dc))
 
-    for g in range(WAVE):
-        send_rows(g)
-    loads[3].wait()
-    found_pick, found_scale = pick_rows(found, mix[...])
-    pick[...] = found_pick
-    scale[...] = found_scale
+    def before_return():
+        loads[3].wait()
+        found_pick, found_scale = pick_rows(found, mix[...])
+        pick[...] = found_pick
+        scale[...] = found_scale
+        loads[4].wait()
+        loads[5].wait()
+
     stages = (stage0, stage1, stage2, stage3, stage4)
-    for s, g in SCHEDULE:
-        if s == LAST:
-            if g == 0:
-                loads[4].wait()
-                loads[5].wait()
+    returning = False
+    for s, g, o in SCHEDULE:
+        if s == ROWS:
+            send_rows(g)
+        elif s == RETURN:
+            if not returning:
+                before_return()
+                returning = True
             stage5(g)
-            continue
-        for o in range(2):
+        else:
             stages[s](g, o)
-        if s == 0 and g + WAVE < GROUPS:
-            send_rows(g + WAVE)
 
     arrive(rows.at[pl.ds(0, (SLOTS - 1) * MOST)], z_send)
     for copy in sends:

time: 100 us -> 97.9 us (0.979)
  Pallas kernels: 97.8 us -> 95.7 us
    pallas_call x1, Pallas kernels: 97.8 us -> 95.7 us  [body(): pl.pallas_call(kernel, out_shape=jax.ShapeDtypeStruct((tok_rows * top, 4...]
where the time goes in v4:
time: 97.9 us; the launch traced here: 97.7 us
  Pallas kernels  95.7 us (98%)
  local copies, waits for them, and re-layouts  2.03 us (2%)
    pallas_call x1, Pallas kernels, body(): pl.pallas_call(kernel, out_shape=jax.ShapeDtypeStruct((tok_rows * top, 4...  95.7 us
    reshape x1, local copies, waits for them, and re-layouts, body(): return weighted.reshape(tok_rows, top, 4 * UNITS)  2.03 us

profile of v4, /device:TPU:1, one launch (start us, length us, event | category | flops | bytes accessed | tf_op | source)
XLA Modules:
  0.0 97.7 jit_solution(13922850136725053421)
XLA Ops:
  0.0 95.7 %shard_map.64 = bf16[256,1024]{1,0:T(8,128)(2,1)} custom-call(bf16[128,384]{1,0:T(8,128)(2,1)} %tokens_hbm.1, bf16[1,3072,256]{2,1,0:T(8,128)(2,1)} %gate_hbm.1, bf16[1,3072,256]{2,1,0:T(8,128)(2,1)} %up_hbm.1, s32[2,128]{1,0:T(2,128)} %bitcast.3, s32[1,16]{1,0:T(1,128)} %bitcast.5, f32[2,128]{1,0:T(2,128)} %bitcast.4), custom_call_target="tpu_custom_call" | custom-call | flops 6442450944 | bytes 4194304 | tf_op jit(solution)/shard_map/pallas_call | solution.py:334
  95.7 2.0 %reshape.7 = bf16[128,2,1024]{2,1,0:T(2,128)(2,1)} reshape(bf16[256,1024]{1,0:T(8,128)(2,1)} %shard_map.64) | data formatting | bytes 1048576 | tf_op jit(solution)/shard_map/reshape | solution.py:371

commit v5 on v4

--- a/solution.py
+++ b/solution.py
@@ -284,10 +284,6 @@
                             remote(src, dst, back_send.at[g], back_recv, ed_device(offset, dh, dc))
 
     def before_return():
-        loads[3].wait()
-        found_pick, found_scale = pick_rows(found, mix[...])
-        pick[...] = found_pick
-        scale[...] = found_scale
         loads[4].wait()
         loads[5].wait()
 
@@ -303,6 +299,11 @@
             stage5(g)
         else:
             stages[s](g, o)
+
+    loads[3].wait()
+    found_pick, found_scale = pick_rows(found, mix[...])
+    pick[...] = found_pick
+    scale[...] = found_scale
 
     arrive(rows.at[pl.ds(0, (SLOTS - 1) * MOST)], z_send)
     for copy in sends:

time: 97.9 us -> 98 us (level)
  no operation moved by 1% of the time
where the time goes in v5:
time: 98 us; the launch traced here: 97.8 us
  Pallas kernels  95.8 us (98%)
  local copies, waits for them, and re-layouts  2.03 us (2%)
    pallas_call x1, Pallas kernels, body(): pl.pallas_call(kernel, out_shape=jax.ShapeDtypeStruct((tok_rows * top, 4...  95.8 us
    reshape x1, local copies, waits for them, and re-layouts, body(): return weighted.reshape(tok_rows, top, 4 * UNITS)  2.03 us

profile of v5, /device:TPU:1, one launch (start us, length us, event | category | flops | bytes accessed | tf_op | source)
XLA Modules:
  0.0 97.8 jit_solution(9588857927072332152)
XLA Ops:
  0.0 95.8 %shard_map.64 = bf16[256,1024]{1,0:T(8,128)(2,1)} custom-call(bf16[128,384]{1,0:T(8,128)(2,1)} %tokens_hbm.1, bf16[1,3072,256]{2,1,0:T(8,128)(2,1)} %gate_hbm.1, bf16[1,3072,256]{2,1,0:T(8,128)(2,1)} %up_hbm.1, s32[2,128]{1,0:T(2,128)} %bitcast.3, s32[1,16]{1,0:T(1,128)} %bitcast.5, f32[2,128]{1,0:T(2,128)} %bitcast.4), custom_call_target="tpu_custom_call" | custom-call | flops 6442450944 | bytes 4194304 | tf_op jit(solution)/shard_map/pallas_call | solution.py:335
  95.8 2.0 %reshape.7 = bf16[128,2,1024]{2,1,0:T(2,128)(2,1)} reshape(bf16[256,1024]{1,0:T(8,128)(2,1)} %shard_map.64) | data formatting | bytes 1048576 | tf_op jit(solution)/shard_map/reshape | solution.py:372
